TPU v7x, 256 devices: a whole 4x4x8 slice. The times are simulated.
256 devices in a mesh: dp: 256 (over x, y, z, core).
Axes of the slice: x: 4, y: 4, z: 8, core: 2. Of those that a mesh axis runs over, the one named last changes fastest.
Arguments:
- pooled: bfloat16 [32768, 1152], P('dp'), may hold values from -6 to 6
- captions: bfloat16 [32768, 1152], P('dp'), may hold values from -0.1796875 to 0.1796875
- norm_gain_vector: float32 [1152], replicated, may hold values from 0.5 to 1.5
- up_matrix: bfloat16 [1152, 2304], replicated, may hold values from -0.1875 to 0.1875
- up_bias_vector: float32 [2304], replicated, may hold values from -3 to 3
- down_matrix: bfloat16 [2304, 1152], replicated, may hold values from -0.125 to 0.125
- log_scale: float32 [1], replicated, may hold values from 1.5 to 2.5
- logit_bias: float32 [1], replicated, may hold values from -4 to -1
Outputs:
- caption_grad: float32 [32768, 1152], P('dp')
- pooled_gradient: float32 [32768, 1152], P('dp')
- gain_grad: float32 [1152], replicated
- up_bias_grad: float32 [2304], P('dp')
All inputs are finite; a program needn't handle non-finite values.
Results may differ from a plain program's by a relative error of at most 0.007.
Values may be sent and summed in bfloat16 or wider, within the bound.
A program may use at most 64 MiB of HBM per device.

v0:
```python
import functools

import jax
import jax.numpy as jnp
from jax import lax
from jax.experimental import pallas as pl
from jax.experimental.pallas import tpu as pltpu
from jax.sharding import PartitionSpec as P

MESH = pl.DeviceIdType.MESH
EPS = 1e-06
CHUNKS = 4
PARTS = 3
NT = (((1,), (1,)), ((), ()))
BEHIND, AHEAD, FAR_BEHIND, FAR_AHEAD, SIBLING, SIB_BEHIND, SIB_AHEAD, SIB_FAR = range(8)


def dot(a, b, dims=(((1,), (0,)), ((), ()))):
    return lax.dot_general(a, b, dims, preferred_element_type=jnp.float32)


def kernel(
    n,
    nz,
    pooled_hbm,
    captions_hbm,
    gain_hbm,
    up_hbm,
    bias_hbm,
    down_hbm,
    scalars,
    caption_out,
    pooled_out,
    gain_out,
    bias_out,
    pooled,
    captions,
    gain,
    up,
    bias,
    down,
    blocks,
    xhat,
    normed,
    slope,
    unit,
    text_unit,
    dembed,
    acc,
    dtext,
    partial,
    plane,
    line,
    caption_sem,
    load_sem,
    send_sem,
    recv_sem,
    plane_send,
    plane_recv,
    line_send,
    line_recv,
):
    rows, width = pooled.shape
    hidden_width = up.shape[1]
    nxy = n // (2 * nz)
    part = rows // CHUNKS
    group = 2 * nz
    slice_width = hidden_width // nxy
    me = lax.axis_index("dp")
    core = lax.rem(me, 2)
    xy = me // (2 * nz)
    sibling = me + 1 - 2 * core
    ahead, behind = lax.rem(me + 2, n), lax.rem(me + n - 2, n)
    plane_peers = [lax.rem(me + 2 * nz * k, n) for k in range(1, nxy)]
    place = lax.rem(me, group)
    line_peers = [xy * group + lax.rem(place + k, group) for k in range(1, group)]

    barrier = pltpu.get_barrier_semaphore()
    greeted = [ahead, behind] + plane_peers + line_peers
    for peer in greeted:
        pl.semaphore_signal(barrier, inc=1, device_id=(peer,), device_id_type=MESH)

    wide = hidden_width // PARTS
    loads = [
        pltpu.make_async_copy(pooled_hbm, pooled, load_sem.at[0]),
        pltpu.make_async_copy(gain_hbm, gain.at[0], load_sem.at[1]),
        pltpu.make_async_copy(bias_hbm, bias.at[0], load_sem.at[2]),
    ]
    up_loads, down_loads = [], []
    for p in range(PARTS):
        span = pl.ds(p * wide, wide)
        up_loads.append(
            pltpu.make_async_copy(up_hbm.at[:, span], up.at[:, span], load_sem.at[3 + 2 * p])
        )
        down_loads.append(
            pltpu.make_async_copy(down_hbm.at[span], down.at[span], load_sem.at[4 + 2 * p])
        )
        loads += [up_loads[-1], down_loads[-1]]
    caption_loads = []
    for c in range(CHUNKS):
        span = pl.ds(c * part, part)
        caption_loads.append(
            pltpu.make_async_copy(captions_hbm.at[span], captions.at[span], caption_sem.at[c])
        )
    for load in caption_loads + loads:
        load.start()

    def move(kind, side, source, target, device, c):
        span = pl.ds(c * part, part)
        return pltpu.make_async_remote_copy(
            src_ref=blocks.at[side, source, span],
            dst_ref=blocks.at[side, target, span],
            send_sem=send_sem.at[side, kind, c],
            recv_sem=recv_sem.at[side, kind, c],
            device_id=(device,),
            device_id_type=MESH,
        )

    def route(kind, side, c):
        if kind == BEHIND:
            return move(kind, side, 4 + core, 2 + core, ahead, c)
        if kind == AHEAD:
            return move(kind, side, 4 + core, 6 + core, behind, c)
        if kind == FAR_BEHIND:
            return move(kind, side, 2 + core, core, ahead, c)
        if kind == FAR_AHEAD:
            return move(kind, side, 6 + core, 8 + core, behind, c)
        if kind == SIBLING:
            return move(kind, side, 4 + core, 4 + core, sibling, c)
        if kind == SIB_BEHIND:
            return move(kind, side, 2 + core, 2 + core, sibling, c)
        if kind == SIB_AHEAD:
            return move(kind, side, 6 + core, 6 + core, sibling, c)
        return move(kind, side, 8 - 7 * core, 8 - 7 * core, sibling, c)

    def start(kinds, side, c):
        for kind in kinds:
            route(kind, side, c).start()

    def arrived(kinds, side, c):
        for kind in kinds:
            route(kind, side, c).wait_recv()

    TEXT, IMAGE = 0, 1
    first, second = range(CHUNKS // 2), range(CHUNKS // 2, CHUNKS)
    text_norms = []
    for c in range(CHUNKS):
        caption_loads[c].wait()
        span = pl.ds(c * part, part)
        text = captions[span].astype(jnp.float32)
        text_norms.append(jnp.sqrt(jnp.sum(text * text, axis=1, keepdims=True) + EPS))
        text_unit[span] = text / text_norms[c]
        blocks[TEXT, 4 + core, span] = text_unit[span].astype(jnp.bfloat16)
        if c == 0:
            pl.semaphore_wait(barrier, len(greeted))
        start([BEHIND, AHEAD] if c in first else [], TEXT, c)
    text_norm = jnp.concatenate(text_norms, axis=0)

    for load in loads[:3]:
        load.wait()
    scale = jnp.exp(jnp.broadcast_to(scalars[0:1, 0:1], (rows, 2 * rows)))
    scale_column = scale[:, :1]
    offset = scalars[1:2, 0:1]
    feats = pooled[...].astype(jnp.float32)
    centered = feats - jnp.mean(feats, axis=1, keepdims=True)
    variance = jnp.mean(centered * centered, axis=1, keepdims=True)
    rstd = lax.rsqrt(variance + EPS)
    xhat[...] = centered * rstd
    normed[...] = (xhat[...] * gain[...]).astype(jnp.bfloat16)
    acc[...] = feats
    for p in range(PARTS):
        span = pl.ds(p * wide, wide)
        up_loads[p].wait()
        x = dot(normed[...], up[:, span]) + bias[:, span]
        c0, c1 = 0.7978845608028654, 0.044715
        square = x * x
        t = jnp.tanh(c0 * x * (1.0 + c1 * square))
        slope[:, span] = 0.5 * (1.0 + t) + (0.5 * c0) * x * (1.0 - t * t) * (
            1.0 + (3.0 * c1) * square
        )
        hidden = (0.5 * x * (1.0 + t)).astype(jnp.bfloat16)
        down_loads[p].wait()
        acc[...] += dot(hidden, down[span])
        if p == 0:
            for c in second:
                start([BEHIND, AHEAD], TEXT, c)
            for c in range(CHUNKS):
                start([SIBLING], TEXT, c)
    embed = acc[...]
    image_norm = jnp.sqrt(jnp.sum(embed * embed, axis=1, keepdims=True) + EPS)
    unit[...] = embed / image_norm
    blocks[IMAGE, 4 + core] = unit[...].astype(jnp.bfloat16)

    def terms(total, side, other, own_chip=False):
        logits = scale[:, : other.shape[0]] * dot(blocks[1 - side, 4 + core], other, NT) + offset
        grad = jax.nn.sigmoid(logits)
        if own_chip:
            same = (
                lax.broadcasted_iota(jnp.int32, logits.shape, 1)
                == lax.broadcasted_iota(jnp.int32, logits.shape, 0) + core * rows
            )
            grad = jnp.where(same, -jax.nn.sigmoid(-logits), grad)
        total[...] += dot(grad.astype(jnp.bfloat16), other)

    def chip(total, side, place, own_chip=False):
        terms(total, side, blocks[side, pl.ds(2 * place, 2)].reshape(2 * rows, width), own_chip)

    def far_line(total, side):
        ends = [blocks[side, core], blocks[side, 8 + core]]
        terms(total, side, jnp.concatenate(ends, axis=0))

    def far_sibling(total, side):
        terms(total, side, blocks[side, 1 + 7 * core])

    def settle(kinds, side):
        for c in range(CHUNKS):
            arrived(kinds, side, c)

    def pass_on(side, chunks):
        for c in chunks:
            arrived([BEHIND, AHEAD], side, c)
            start([FAR_BEHIND, FAR_AHEAD, SIB_BEHIND, SIB_AHEAD], side, c)

    acc[...] = jnp.zeros_like(acc)
    pass_on(TEXT, first)
    for c in range(CHUNKS):
        start([SIBLING], IMAGE, c)
    settle([SIBLING], TEXT)
    chip(acc, TEXT, 2, True)
    pass_on(TEXT, second)
    settle([SIB_BEHIND, SIB_AHEAD], TEXT)
    chip(acc, TEXT, 1)
    chip(acc, TEXT, 3)
    for c in range(CHUNKS):
        for kind in (FAR_BEHIND, FAR_AHEAD):
            route(kind, TEXT, c).wait_send()
    for c in first:
        start([BEHIND, AHEAD], IMAGE, c)
    for c in range(CHUNKS):
        arrived([FAR_BEHIND, FAR_AHEAD], TEXT, c)
        start([SIB_FAR], TEXT, c)
    far_line(acc, TEXT)
    settle([SIB_FAR], TEXT)
    far_sibling(acc, TEXT)
    for c in second:
        start([BEHIND, AHEAD], IMAGE, c)

    dimage = scale_column * acc[...]
    along = jnp.sum(unit[...] * dimage, axis=1, keepdims=True)
    dembed[...] = ((dimage - unit[...] * along) / image_norm).astype(jnp.bfloat16)
    acc[...] = jnp.zeros_like(acc)
    bias_parts = bias
    for p in range(PARTS):
        span = pl.ds(p * wide, wide)
        dpre = (dot(dembed[...], down[span], NT) * slope[:, span]).astype(jnp.bfloat16)
        bias_parts[:, span] = jnp.sum(dpre.astype(jnp.float32), axis=0, keepdims=True)
        acc[...] += dot(dpre, up[:, span], NT)
        if p == 1:
            pass_on(IMAGE, first)

    partial[:, :, :width] = jnp.broadcast_to(
        jnp.sum(acc[...] * xhat[...], axis=0, keepdims=True)[None], (nxy, 1, width)
    )
    for q in range(nxy):
        partial[q, :, width : width + slice_width] = bias_parts[
            :, q * slice_width : (q + 1) * slice_width
        ]

    def in_plane(k):
        return pltpu.make_async_remote_copy(
            src_ref=partial.at[lax.rem(xy + k + 1, nxy)],
            dst_ref=plane.at[xy],
            send_sem=plane_send.at[k],
            recv_sem=plane_recv.at[k],
            device_id=(plane_peers[k],),
            device_id_type=MESH,
        )

    def in_line(k):
        return pltpu.make_async_remote_copy(
            src_ref=line.at[place],
            dst_ref=line.at[place],
            send_sem=line_send.at[k],
            recv_sem=line_recv.at[k],
            device_id=(line_peers[k],),
            device_id_type=MESH,
        )

    for k in range(nxy - 1):
        in_plane(k).start()
    plane[xy] = partial[xy]

    dxhat = acc[...] * gain[...]
    mean1 = jnp.mean(dxhat, axis=1, keepdims=True)
    mean2 = jnp.mean(dxhat * xhat[...], axis=1, keepdims=True)
    pooled_out[...] = dembed[...].astype(jnp.float32) + rstd * (
        dxhat - mean1 - xhat[...] * mean2
    )
    dtext[...] = jnp.zeros_like(dtext)
    settle([SIBLING], IMAGE)
    chip(dtext, IMAGE, 2, True)
    pass_on(IMAGE, second)
    settle([SIB_BEHIND, SIB_AHEAD], IMAGE)
    chip(dtext, IMAGE, 1)
    chip(dtext, IMAGE, 3)

    for k in range(nxy - 1):
        in_plane(k).wait_recv()
    line[place] = jnp.sum(plane[...], axis=0)
    for k in range(group - 1):
        in_line(k).start()

    for c in range(CHUNKS):
        arrived([FAR_BEHIND, FAR_AHEAD], IMAGE, c)
        start([SIB_FAR], IMAGE, c)
    far_line(dtext, IMAGE)
    settle([SIB_FAR], IMAGE)
    far_sibling(dtext, IMAGE)

    dcaption = scale_column * dtext[...]
    along = jnp.sum(text_unit[...] * dcaption, axis=1, keepdims=True)
    caption_out[...] = (dcaption - text_unit[...] * along) / text_norm

    for k in range(group - 1):
        in_line(k).wait_recv()
    summed = jnp.sum(line[...], axis=0)
    gain_out[...] = summed[:, :width]
    bias_out[...] = summed[:, width:]

    for side in (TEXT, IMAGE):
        for kind in range(8):
            for c in range(CHUNKS):
                if side == IMAGE or kind not in (FAR_BEHIND, FAR_AHEAD):
                    route(kind, side, c).wait_send()
    for k in range(nxy - 1):
        in_plane(k).wait_send()
    for k in range(group - 1):
        in_line(k).wait_send()


def finish(group, caption, pooled, gain, bias, caption_out, pooled_out, gain_out, bias_out, sems):
    share = bias_out.shape[0]
    part = caption.shape[0] // CHUNKS
    copies = [pltpu.make_async_copy(gain.at[0], gain_out, sems.at[2 * CHUNKS])]
    for c in range(CHUNKS):
        span = pl.ds(c * part, part)
        copies += [
            pltpu.make_async_copy(caption.at[span], caption_out.at[span], sems.at[2 * c]),
            pltpu.make_async_copy(pooled.at[span], pooled_out.at[span], sems.at[2 * c + 1]),
        ]
    for copy in copies:
        copy.start()
    total = bias.shape[1]
    begin = lax.rem(lax.axis_index("dp"), group) * share
    turned = pltpu.roll(bias[...], lax.rem(total - begin, total), 1)
    bias_out[...] = turned[0, :share]
    for copy in copies:
        copy.wait()


def local(
    n,
    nz,
    pooled,
    captions,
    norm_gain_vector,
    up_matrix,
    up_bias_vector,
    down_matrix,
    log_scale,
    logit_bias,
):
    rows, width = pooled.shape
    hidden_width = up_matrix.shape[1]
    nxy = n // (2 * nz)
    slice_width = -(-hidden_width // nxy // 128) * 128
    f32, bf16 = jnp.float32, jnp.bfloat16
    vmem = pl.BlockSpec(memory_space=pltpu.VMEM)
    away = pl.BlockSpec(memory_space=pltpu.HBM)
    dma = pltpu.SemaphoreType.DMA
    caption_grad, pooled_gradient, gain_grad, bias_whole = pl.pallas_call(
        functools.partial(kernel, n, nz),
        out_shape=(
            jax.ShapeDtypeStruct((rows, width), f32),
            jax.ShapeDtypeStruct((rows, width), f32),
            jax.ShapeDtypeStruct((1, width), f32),
            jax.ShapeDtypeStruct((1, slice_width), f32),
        ),
        in_specs=[away] * 6 + [vmem],
        out_specs=(vmem,) * 4,
        scratch_shapes=[
            pltpu.VMEM((rows, width), bf16),
            pltpu.VMEM((rows, width), bf16),
            pltpu.VMEM((1, width), f32),
            pltpu.VMEM((width, hidden_width), bf16),
            pltpu.VMEM((1, hidden_width), f32),
            pltpu.VMEM((hidden_width, width), bf16),
            pltpu.VMEM((2, 10, rows, width), bf16),
            pltpu.VMEM((rows, width), f32),
            pltpu.VMEM((rows, width), bf16),
            pltpu.VMEM((rows, hidden_width), f32),
            pltpu.VMEM((rows, width), f32),
            pltpu.VMEM((rows, width), f32),
            pltpu.VMEM((rows, width), bf16),
            pltpu.VMEM((rows, width), f32),
            pltpu.VMEM((rows, width), f32),
            pltpu.VMEM((nxy, 1, width + slice_width), f32),
            pltpu.VMEM((nxy, 1, width + slice_width), f32),
            pltpu.VMEM((2 * nz, 1, width + slice_width), f32),
            dma((CHUNKS,)),
            dma((3 + 2 * PARTS,)),
            dma((2, 8, CHUNKS)),
            dma((2, 8, CHUNKS)),
            dma((nxy - 1,)),
            dma((nxy - 1,)),
            dma((2 * nz - 1,)),
            dma((2 * nz - 1,)),
        ],
        compiler_params=pltpu.CompilerParams(
            collective_id=0, has_side_effects=True, vmem_limit_bytes=48 * 2**20
        ),
    )(
        *(
            pltpu.with_memory_space_constraint(array, pltpu.HBM)
            for array in (
                pooled,
                captions,
                norm_gain_vector,
                up_matrix,
                up_bias_vector,
                down_matrix,
            )
        ),
        jnp.where(lax.broadcasted_iota(jnp.int32, (2, 128), 0) == 0, log_scale, logit_bias),
    )
    return pl.pallas_call(
        functools.partial(finish, 2 * nz),
        out_shape=(
            jax.ShapeDtypeStruct((rows, width), f32),
            jax.ShapeDtypeStruct((rows, width), f32),
            jax.ShapeDtypeStruct((width,), f32),
            jax.ShapeDtypeStruct((hidden_width // n,), f32),
        ),
        in_specs=[vmem] * 4,
        out_specs=(away, away, away, vmem),
        scratch_shapes=[dma((2 * CHUNKS + 1,))],
        compiler_params=pltpu.CompilerParams(vmem_limit_bytes=4 * 2**20),
    )(caption_grad, pooled_gradient, gain_grad, bias_whole)


def solution(mesh, nz=8):
    placed = (P("dp", None), P("dp", None), P(), P(), P(), P(), P(), P())
    return jax.shard_map(
        functools.partial(local, mesh.shape["dp"], nz),
        mesh=mesh,
        in_specs=placed,
        out_specs=(P("dp", None), P("dp", None), P(), P("dp")),
        check_vma=False,
    )
```

profile of v0, /device:TPU:1, one launch (start us, length us, event | category | flops | bytes accessed | tf_op | source)
XLA Modules:
  0.0 53.8 jit_solution(12555778105690085165)
XLA Ops:
  1.9 0.1 iota.7.scalars
  2.0 50.2 %shard_map.117 = (f32[128,1152]{1,0:T(8,128)S(1)}, f32[128,1152]{1,0:T(8,128)S(1)}, f32[1,1152]{1,0:T(1,128)S(1)}, f32[1,256]{1,0:T(1,128)S(1)}) custom-call(bf16[128,1152]{1,0:T(8,128)(2,1)} %pooled_hbm.1, bf16[128,1152]{1,0:T(8,128)(2,1)} %captions_hbm.1, f32[1152]{0:T(1024)} %gain_hbm.1, bf16[1152,2304]{1,0:T(8,128)(2,1)} %up_hbm.1, f32[2304]{0:T(1024)} %bias_hbm.1, ...), custom_call_target="tpu_custom_call" | custom-call | tf_op jit(solution)/shard_map/pallas_call | solution.py:381
  52.2 1.6 %shard_map.118 = (f32[128,1152]{1,0:T(8,128)}, f32[128,1152]{1,0:T(8,128)}, f32[1152]{0:T(1024)}, f32[9]{0:T(128)}) custom-call(f32[128,1152]{1,0:T(8,128)S(1)} %get-tuple-element.8.caption, f32[128,1152]{1,0:T(8,128)S(1)} %get-tuple-element.9.pooled, f32[1,1152]{1,0:T(1,128)S(1)} %get-tuple-element.10.gain, f32[1,256]{1,0:T(1,128)S(1)} %get-tuple-element.11.bias), custom_call_target="tpu_custom_call" | custom-call | tf_op jit(solution)/shard_map/pallas_call | solution.py:436
  (1 shorter events, 0.0 us)
where the time goes:
time: 53.9 us; the launch traced here: 53.8 us
  Pallas kernels  51.8 us (96%)
  between operations  1.94 us (4%)
    pallas_call x1, Pallas kernels, local(): pl.pallas_call(functools.partial(kernel, n, nz), out_shape=(jax.ShapeDtyp...  50.2 us
    pallas_call x1, Pallas kernels, local(): pl.pallas_call(functools.partial(finish, 2 * nz), out_shape=(jax.ShapeDty...  1.6 us

commit v1 on v0

--- a/solution.py
+++ b/solution.py
@@ -39,6 +39,8 @@
     up,
     bias,
     down,
+    up_turned,
+    down_turned,
     blocks,
     xhat,
     normed,
@@ -218,8 +220,11 @@
 
     def pass_on(side, chunks):
         for c in chunks:
-            arrived([BEHIND, AHEAD], side, c)
-            start([FAR_BEHIND, FAR_AHEAD, SIB_BEHIND, SIB_AHEAD], side, c)
+            arrived([BEHIND], side, c)
+            start([FAR_BEHIND, SIB_BEHIND], side, c)
+        for c in chunks:
+            arrived([AHEAD], side, c)
+            start([FAR_AHEAD, SIB_AHEAD], side, c)
 
     acc[...] = jnp.zeros_like(acc)
     pass_on(TEXT, first)
@@ -231,10 +236,16 @@
     settle([SIB_BEHIND, SIB_AHEAD], TEXT)
     chip(acc, TEXT, 1)
     chip(acc, TEXT, 3)
-    for c in range(CHUNKS):
-        for kind in (FAR_BEHIND, FAR_AHEAD):
-            route(kind, TEXT, c).wait_send()
-    for c in first:
+    for q in range(0, width, rows):
+        up_turned[:, q : q + rows] = up[q : q + rows].T
+    for kind, far in ((BEHIND, FAR_BEHIND), (AHEAD, FAR_AHEAD)):
+        for c in range(CHUNKS):
+            route(far, TEXT, c).wait_send()
+        for c in first:
+            start([kind], IMAGE, c)
+    for q in range(0, hidden_width, rows):
+        down_turned[:, q : q + rows] = down[q : q + rows].T
+    for c in second:
         start([BEHIND, AHEAD], IMAGE, c)
     for c in range(CHUNKS):
         arrived([FAR_BEHIND, FAR_AHEAD], TEXT, c)
@@ -242,21 +253,18 @@
     far_line(acc, TEXT)
     settle([SIB_FAR], TEXT)
     far_sibling(acc, TEXT)
-    for c in second:
-        start([BEHIND, AHEAD], IMAGE, c)
 
     dimage = scale_column * acc[...]
     along = jnp.sum(unit[...] * dimage, axis=1, keepdims=True)
     dembed[...] = ((dimage - unit[...] * along) / image_norm).astype(jnp.bfloat16)
     acc[...] = jnp.zeros_like(acc)
+    pass_on(IMAGE, first)
     bias_parts = bias
     for p in range(PARTS):
         span = pl.ds(p * wide, wide)
-        dpre = (dot(dembed[...], down[span], NT) * slope[:, span]).astype(jnp.bfloat16)
+        dpre = (dot(dembed[...], down_turned[:, span]) * slope[:, span]).astype(jnp.bfloat16)
         bias_parts[:, span] = jnp.sum(dpre.astype(jnp.float32), axis=0, keepdims=True)
-        acc[...] += dot(dpre, up[:, span], NT)
-        if p == 1:
-            pass_on(IMAGE, first)
+        acc[...] += dot(dpre, up_turned[span])
 
     partial[:, :, :width] = jnp.broadcast_to(
         jnp.sum(acc[...] * xhat[...], axis=0, keepdims=True)[None], (nxy, 1, width)
@@ -289,6 +297,7 @@
     for k in range(nxy - 1):
         in_plane(k).start()
     plane[xy] = partial[xy]
+    pass_on(IMAGE, second)
 
     dxhat = acc[...] * gain[...]
     mean1 = jnp.mean(dxhat, axis=1, keepdims=True)
@@ -299,7 +308,6 @@
     dtext[...] = jnp.zeros_like(dtext)
     settle([SIBLING], IMAGE)
     chip(dtext, IMAGE, 2, True)
-    pass_on(IMAGE, second)
     settle([SIB_BEHIND, SIB_AHEAD], IMAGE)
     chip(dtext, IMAGE, 1)
     chip(dtext, IMAGE, 3)
@@ -395,6 +403,8 @@
             pltpu.VMEM((width, hidden_width), bf16),
             pltpu.VMEM((1, hidden_width), f32),
             pltpu.VMEM((hidden_width, width), bf16),
+            pltpu.VMEM((hidden_width, width), bf16),
+            pltpu.VMEM((width, hidden_width), bf16),
             pltpu.VMEM((2, 10, rows, width), bf16),
             pltpu.VMEM((rows, width), f32),
             pltpu.VMEM((rows, width), bf16),

time: 53.9 us -> 50.8 us (0.942)
  Pallas kernels: 51.8 us -> 48.7 us
    pallas_call x1, Pallas kernels: 50.2 us -> 47.1 us  [local(): pl.pallas_call(functools.partial(kernel, n, nz), out_shape=(jax.ShapeDtyp...]
where the time goes in v1:
time: 50.8 us; the launch traced here: 50.7 us
  Pallas kernels  48.7 us (96%)
  between operations  1.94 us (4%)
    pallas_call x1, Pallas kernels, local(): pl.pallas_call(functools.partial(kernel, n, nz), out_shape=(jax.ShapeDtyp...  47.1 us
    pallas_call x1, Pallas kernels, local(): pl.pallas_call(functools.partial(finish, 2 * nz), out_shape=(jax.ShapeDty...  1.6 us

profile of v1, /device:TPU:1, one launch (start us, length us, event | category | flops | bytes accessed | tf_op | source)
XLA Modules:
  0.0 50.7 jit_solution(2329807227403467089)
XLA Ops:
  1.9 0.1 iota.7.scalars
  2.0 47.1 %shard_map.117 = (f32[128,1152]{1,0:T(8,128)S(1)}, f32[128,1152]{1,0:T(8,128)S(1)}, f32[1,1152]{1,0:T(1,128)S(1)}, f32[1,256]{1,0:T(1,128)S(1)}) custom-call(bf16[128,1152]{1,0:T(8,128)(2,1)} %pooled_hbm.1, bf16[128,1152]{1,0:T(8,128)(2,1)} %captions_hbm.1, f32[1152]{0:T(1024)} %gain_hbm.1, bf16[1152,2304]{1,0:T(8,128)(2,1)} %up_hbm.1, f32[2304]{0:T(1024)} %bias_hbm.1, ...), custom_call_target="tpu_custom_call" | custom-call | tf_op jit(solution)/shard_map/pallas_call | solution.py:389
  49.1 1.6 %shard_map.118 = (f32[128,1152]{1,0:T(8,128)}, f32[128,1152]{1,0:T(8,128)}, f32[1152]{0:T(1024)}, f32[9]{0:T(128)}) custom-call(f32[128,1152]{1,0:T(8,128)S(1)} %get-tuple-element.8.caption, f32[128,1152]{1,0:T(8,128)S(1)} %get-tuple-element.9.pooled, f32[1,1152]{1,0:T(1,128)S(1)} %get-tuple-element.10.gain, f32[1,256]{1,0:T(1,128)S(1)} %get-tuple-element.11.bias), custom_call_target="tpu_custom_call" | custom-call | tf_op jit(solution)/shard_map/pallas_call | solution.py:446
  (1 shorter events, 0.0 us)

commit v2 on v1

--- a/solution.py
+++ b/solution.py
@@ -73,6 +73,12 @@
     xy = me // (2 * nz)
     sibling = me + 1 - 2 * core
     ahead, behind = lax.rem(me + 2, n), lax.rem(me + n - 2, n)
+
+    def onward(k):
+        return lax.rem(me + 2 + k * (n - 4), n)
+
+    prompt = 1 - lax.rem(me // 2, nz) // (nz // 2)
+    order = (prompt, 1 - prompt)
     plane_peers = [lax.rem(me + 2 * nz * k, n) for k in range(1, nxy)]
     place = lax.rem(me, group)
     line_peers = [xy * group + lax.rem(place + k, group) for k in range(1, group)]
@@ -118,21 +124,24 @@
             device_id_type=MESH,
         )
 
+    def near(k, side, c):
+        return move(BEHIND + k, side, 4 + core, 2 + 4 * k + core, onward(k), c)
+
+    def far(k, side, c):
+        return move(FAR_BEHIND + k, side, 2 + 4 * k + core, 8 * k + core, onward(k), c)
+
+    def near_to_sibling(k, side, c):
+        return move(SIB_BEHIND + k, side, 2 + 4 * k + core, 2 + 4 * k + core, sibling, c)
+
     def route(kind, side, c):
-        if kind == BEHIND:
-            return move(kind, side, 4 + core, 2 + core, ahead, c)
-        if kind == AHEAD:
-            return move(kind, side, 4 + core, 6 + core, behind, c)
-        if kind == FAR_BEHIND:
-            return move(kind, side, 2 + core, core, ahead, c)
-        if kind == FAR_AHEAD:
-            return move(kind, side, 6 + core, 8 + core, behind, c)
+        if kind in (BEHIND, AHEAD):
+            return near(kind - BEHIND, side, c)
+        if kind in (FAR_BEHIND, FAR_AHEAD):
+            return far(kind - FAR_BEHIND, side, c)
+        if kind in (SIB_BEHIND, SIB_AHEAD):
+            return near_to_sibling(kind - SIB_BEHIND, side, c)
         if kind == SIBLING:
             return move(kind, side, 4 + core, 4 + core, sibling, c)
-        if kind == SIB_BEHIND:
-            return move(kind, side, 2 + core, 2 + core, sibling, c)
-        if kind == SIB_AHEAD:
-            return move(kind, side, 6 + core, 6 + core, sibling, c)
         return move(kind, side, 8 - 7 * core, 8 - 7 * core, sibling, c)
 
     def start(kinds, side, c):
@@ -214,17 +223,21 @@
     def far_sibling(total, side):
         terms(total, side, blocks[side, 1 + 7 * core])
 
+    def left(kinds, side):
+        for kind in kinds:
+            for c in range(CHUNKS):
+                route(kind, side, c).wait_send()
+
     def settle(kinds, side):
         for c in range(CHUNKS):
             arrived(kinds, side, c)
 
-    def pass_on(side, chunks):
-        for c in chunks:
-            arrived([BEHIND], side, c)
-            start([FAR_BEHIND, SIB_BEHIND], side, c)
-        for c in chunks:
-            arrived([AHEAD], side, c)
-            start([FAR_AHEAD, SIB_AHEAD], side, c)
+    def pass_on(side, chunks, directions=order):
+        for k in directions:
+            for c in chunks:
+                near(k, side, c).wait_recv()
+                far(k, side, c).start()
+                near_to_sibling(k, side, c).start()
 
     acc[...] = jnp.zeros_like(acc)
     pass_on(TEXT, first)
@@ -233,20 +246,25 @@
     settle([SIBLING], TEXT)
     chip(acc, TEXT, 2, True)
     pass_on(TEXT, second)
+    for k in order:
+        near(k, IMAGE, 0).start()
     settle([SIB_BEHIND, SIB_AHEAD], TEXT)
     chip(acc, TEXT, 1)
     chip(acc, TEXT, 3)
     for q in range(0, width, rows):
         up_turned[:, q : q + rows] = up[q : q + rows].T
-    for kind, far in ((BEHIND, FAR_BEHIND), (AHEAD, FAR_AHEAD)):
-        for c in range(CHUNKS):
-            route(far, TEXT, c).wait_send()
-        for c in first:
-            start([kind], IMAGE, c)
+    for c in range(CHUNKS):
+        far(prompt, TEXT, c).wait_send()
+    near(prompt, IMAGE, 1).start()
     for q in range(0, hidden_width, rows):
         down_turned[:, q : q + rows] = down[q : q + rows].T
     for c in second:
-        start([BEHIND, AHEAD], IMAGE, c)
+        near(prompt, IMAGE, c).start()
+    for c in range(CHUNKS):
+        far(1 - prompt, TEXT, c).wait_send()
+    for c in range(1, CHUNKS):
+        near(1 - prompt, IMAGE, c).start()
+    pass_on(IMAGE, first, order[:1])
     for c in range(CHUNKS):
         arrived([FAR_BEHIND, FAR_AHEAD], TEXT, c)
         start([SIB_FAR], TEXT, c)
@@ -258,7 +276,6 @@
     along = jnp.sum(unit[...] * dimage, axis=1, keepdims=True)
     dembed[...] = ((dimage - unit[...] * along) / image_norm).astype(jnp.bfloat16)
     acc[...] = jnp.zeros_like(acc)
-    pass_on(IMAGE, first)
     bias_parts = bias
     for p in range(PARTS):
         span = pl.ds(p * wide, wide)
@@ -297,6 +314,7 @@
     for k in range(nxy - 1):
         in_plane(k).start()
     plane[xy] = partial[xy]
+    pass_on(IMAGE, first, order[1:])
     pass_on(IMAGE, second)
 
     dxhat = acc[...] * gain[...]
@@ -318,6 +336,10 @@
     for k in range(group - 1):
         in_line(k).start()
 
+    left([BEHIND, AHEAD, SIBLING, SIB_BEHIND, SIB_AHEAD, SIB_FAR], TEXT)
+    left([BEHIND, AHEAD, SIBLING, SIB_BEHIND, SIB_AHEAD], IMAGE)
+    for k in range(nxy - 1):
+        in_plane(k).wait_send()
     for c in range(CHUNKS):
         arrived([FAR_BEHIND, FAR_AHEAD], IMAGE, c)
         start([SIB_FAR], IMAGE, c)
@@ -335,35 +357,21 @@
     gain_out[...] = summed[:, :width]
     bias_out[...] = summed[:, width:]
 
-    for side in (TEXT, IMAGE):
-        for kind in range(8):
-            for c in range(CHUNKS):
-                if side == IMAGE or kind not in (FAR_BEHIND, FAR_AHEAD):
-                    route(kind, side, c).wait_send()
-    for k in range(nxy - 1):
-        in_plane(k).wait_send()
+    for kind in (FAR_BEHIND, FAR_AHEAD, SIB_FAR):
+        left([kind], IMAGE)
     for k in range(group - 1):
         in_line(k).wait_send()
 
 
-def finish(group, caption, pooled, gain, bias, caption_out, pooled_out, gain_out, bias_out, sems):
+def finish(group, caption, pooled, gain, bias, caption_out, pooled_out, gain_out, bias_out):
     share = bias_out.shape[0]
-    part = caption.shape[0] // CHUNKS
-    copies = [pltpu.make_async_copy(gain.at[0], gain_out, sems.at[2 * CHUNKS])]
-    for c in range(CHUNKS):
-        span = pl.ds(c * part, part)
-        copies += [
-            pltpu.make_async_copy(caption.at[span], caption_out.at[span], sems.at[2 * c]),
-            pltpu.make_async_copy(pooled.at[span], pooled_out.at[span], sems.at[2 * c + 1]),
-        ]
-    for copy in copies:
-        copy.start()
+    caption_out[...] = caption[...]
+    pooled_out[...] = pooled[...]
+    gain_out[...] = gain[0, :]
     total = bias.shape[1]
     begin = lax.rem(lax.axis_index("dp"), group) * share
     turned = pltpu.roll(bias[...], lax.rem(total - begin, total), 1)
     bias_out[...] = turned[0, :share]
-    for copy in copies:
-        copy.wait()
 
 
 def local(
@@ -452,9 +460,8 @@
             jax.ShapeDtypeStruct((hidden_width // n,), f32),
         ),
         in_specs=[vmem] * 4,
-        out_specs=(away, away, away, vmem),
-        scratch_shapes=[dma((2 * CHUNKS + 1,))],
-        compiler_params=pltpu.CompilerParams(vmem_limit_bytes=4 * 2**20),
+        out_specs=(vmem,) * 4,
+        compiler_params=pltpu.CompilerParams(vmem_limit_bytes=8 * 2**20),
     )(caption_grad, pooled_gradient, gain_grad, bias_whole)
 
 

time: 50.8 us -> 50.3 us (level)
    pallas_call x1, Pallas kernels: 1.6 us -> 1.05 us  [local(): pl.pallas_call(functools.partial(finish, 2 * nz), out_shape=(jax.ShapeDty...]
where the time goes in v2:
time: 50.3 us; the launch traced here: 50.2 us
  Pallas kernels  48.2 us (96%)
  between operations  1.94 us (4%)
    pallas_call x1, Pallas kernels, local(): pl.pallas_call(functools.partial(kernel, n, nz), out_shape=(jax.ShapeDtyp...  47.1 us
    pallas_call x1, Pallas kernels, local(): pl.pallas_call(functools.partial(finish, 2 * nz), out_shape=(jax.ShapeDty...  1.05 us

profile of v2, /device:TPU:1, one launch (start us, length us, event | category | flops | bytes accessed | tf_op | source)
XLA Modules:
  0.0 50.2 jit_solution(15508249017062736439)
XLA Ops:
  1.9 0.1 iota.7.scalars
  2.0 47.1 %shard_map.117 = (f32[128,1152]{1,0:T(8,128)S(1)}, f32[128,1152]{1,0:T(8,128)S(1)}, f32[1,1152]{1,0:T(1,128)S(1)}, f32[1,256]{1,0:T(1,128)S(1)}) custom-call(bf16[128,1152]{1,0:T(8,128)(2,1)} %pooled_hbm.1, bf16[128,1152]{1,0:T(8,128)(2,1)} %captions_hbm.1, f32[1152]{0:T(1024)} %gain_hbm.1, bf16[1152,2304]{1,0:T(8,128)(2,1)} %up_hbm.1, f32[2304]{0:T(1024)} %bias_hbm.1, ...), custom_call_target="tpu_custom_call" | custom-call | tf_op jit(solution)/shard_map/pallas_call | solution.py:397
  49.1 1.1 %shard_map.118 = (f32[128,1152]{1,0:T(8,128)}, f32[128,1152]{1,0:T(8,128)}, f32[1152]{0:T(1024)}, f32[9]{0:T(128)}) custom-call(f32[128,1152]{1,0:T(8,128)S(1)} %get-tuple-element.8.caption, f32[128,1152]{1,0:T(8,128)S(1)} %get-tuple-element.9.pooled, f32[1,1152]{1,0:T(1,128)S(1)} %get-tuple-element.10.gain, f32[1,256]{1,0:T(1,128)S(1)} %get-tuple-element.11.bias), custom_call_target="tpu_custom_call" | custom-call | tf_op jit(solution)/shard_map/pallas_call | solution.py:454
  (1 shorter events, 0.0 us)
